TPU v7x, 256 devices: a whole 4x4x8 slice. The times are simulated.
256 devices in a mesh: wide: 64 (over x_lo, y, z), head: 4 (over x_hi, core).
Axes of the slice: x: 4 (x_hi: 2, x_lo: 2; x = x_hi * 2 + x_lo), y: 4, z: 8, core: 2. Of those that a mesh axis runs over, the one named last changes fastest.
Arguments:
- queries: bfloat16 [24576, 4096], P('wide', 'head'), may hold values from -200 to 200
- keys: bfloat16 [4096, 4096], P('wide', 'head'), may hold values from -16 to 16
- values: bfloat16 [4096, 4096], P('wide', 'head'), may hold values from -24 to 24
- frame_mask: int32 [24576, 64], P('wide'), may hold values from 0 to 1, as said below
- frame_slot: int32 [64], replicated, may hold values from 0 to 63, each once
- out_weight: bfloat16 [4096, 4096], P('head', 'wide'), may hold values from -0.09375 to 0.09375
- residual: bfloat16 [24576, 4096], P('wide', 'head'), may hold values from -3 to 3
- gate: float32 [4096], P('head'), may hold values from -1.5 to 1.5
Outputs:
- updated: bfloat16 [24576, 4096], P('wide', 'head')
Inputs may be any that keep to these rules, and one draw needn't show every extreme that they name: `frame_mask`: row r sees exactly the frames whose ids lie below a bound of its own, from 0 to 64.
All inputs are finite; a program needn't handle non-finite values.
Results may differ from a plain program's by a relative error of at most 0.0065.
Values may be sent and summed in bfloat16 or wider, within the bound.
A program may use at most 128 MiB of HBM per device.

v0:
```python
import math

import jax
import jax.numpy as jnp
from jax import lax
from jax.sharding import PartitionSpec as P

HSIZE = 128
TOKF = 64


def on_device(queries, keys, values, frame_mask, frame_slot, out_weight, residual, gate):
    row_count = queries.shape[0]
    head_count = queries.shape[1] // HSIZE
    query_rows = queries.reshape(row_count, head_count, HSIZE)
    frame_count = frame_mask.shape[1]
    mask_float = frame_mask.astype(jnp.float32)
    score_scale = 1.0 / math.sqrt(HSIZE)
    frame_ids = jnp.arange(frame_count, dtype=jnp.int32)

    def attend_block(running, key_rows, value_rows, offset):
        run_max, run_total, run_acc = running
        key_count = key_rows.shape[0]
        slot_of = (offset + jnp.arange(key_count, dtype=jnp.int32)) // TOKF
        slot_match = (slot_of[:, None] == frame_ids[None, :]).astype(jnp.int32)
        frame_of = jnp.sum(slot_match * frame_slot[None, :], axis=1)
        select = (frame_ids[:, None] == frame_of[None, :]).astype(jnp.float32)
        visible = jnp.dot(mask_float, select, precision=lax.Precision.HIGHEST) > 0.5
        key_block = key_rows.reshape(key_count, head_count, HSIZE)
        value_block = value_rows.reshape(key_count, head_count, HSIZE)
        scores = (
            jnp.einsum("rhd,thd->rht", query_rows, key_block, preferred_element_type=jnp.float32)
            * score_scale
        )
        seen_mask = visible[:, None, :]
        block_max = jnp.max(jnp.where(seen_mask, scores, -1e30), axis=2)
        new_max = jnp.maximum(run_max, block_max)
        weights = jnp.exp(jnp.where(seen_mask, scores - new_max[:, :, None], -1e30))
        factor = jnp.exp(run_max - new_max)
        run_total = run_total * factor + jnp.sum(weights, axis=2)
        mixed = jnp.einsum(
            "rht,thd->rhd",
            weights.astype(jnp.bfloat16),
            value_block,
            preferred_element_type=jnp.float32,
        )
        run_acc = run_acc * factor[:, :, None] + mixed
        return (new_max, run_total, run_acc)

    initial = (
        jnp.full((row_count, head_count), -1e30, jnp.float32),
        jnp.zeros((row_count, head_count), jnp.float32),
        jnp.zeros((row_count, head_count, HSIZE), jnp.float32),
    )
    all_keys, all_values = (
        lax.all_gather(keys, "wide", axis=0, tiled=True),
        lax.all_gather(values, "wide", axis=0, tiled=True),
    )
    running = initial
    piece_rows = all_keys.shape[0]
    block_size = math.gcd(piece_rows, 512)
    block_count = piece_rows // block_size

    def inner(state, block_index):
        offset = block_index * block_size
        key_rows = lax.dynamic_slice_in_dim(all_keys, offset, block_size, 0)
        value_rows = lax.dynamic_slice_in_dim(all_values, offset, block_size, 0)
        return (attend_block(state, key_rows, value_rows, offset), None)

    running, _ = lax.scan(inner, running, jnp.arange(block_count, dtype=jnp.int32))
    run_max, run_total, run_acc = running
    seen_count = jnp.sum(frame_mask, axis=1)
    divisor = run_total + (seen_count == 0).astype(jnp.float32)[:, None]
    attended = (
        (run_acc / divisor[:, :, None]).reshape(row_count, head_count * HSIZE).astype(jnp.bfloat16)
    )
    partial_terms = jnp.dot(
        attended,
        lax.all_gather(out_weight, "wide", axis=1, tiled=True),
        preferred_element_type=jnp.float32,
    )
    col_count = residual.shape[1]
    summed = lax.psum(partial_terms, "head")
    own_part = lax.dynamic_slice_in_dim(summed, lax.axis_index("head") * col_count, col_count, 1)
    updated = residual.astype(jnp.float32) + jnp.tanh(gate)[None, :] * own_part
    return updated.astype(jnp.bfloat16)


def solution(mesh):
    return jax.shard_map(
        on_device,
        mesh=mesh,
        in_specs=(
            P("wide", "head"),
            P("wide", "head"),
            P("wide", "head"),
            P("wide", None),
            P(),
            P("head", "wide"),
            P("wide", "head"),
            P("head"),
        ),
        out_specs=P("wide", "head"),
        check_vma=False,
    )
```

profile of v0, /device:TPU:1, one launch (start us, length us, event | category | flops | bytes accessed | tf_op | source)
XLA Modules:
  0.0 1095.8 jit_solution(8689112697533577121)
XLA Ops:
  6.5 0.7 all-gather.4.cloned.1.call-update
  7.3 0.7 all-gather.6.cloned.1.call-update
  8.1 0.7 all-gather.8.cloned.1.call-update
  8.8 1.0 copy.28
  9.8 0.9 reduce_sum.33
  10.8 1.5 copy.29
  12.3 1.2 copy.31
  13.4 0.7 convert_element_type.31
  14.1 273.6 %all-gather.4.cloned.1.call-done = bf16[4096,1024]{1,0:T(8,128)(2,1)} async-done(((bf16[64,1024]{1,0:T(8,128)(2,1)}), bf16[4096,1024]{1,0:T(8,128)(2,1)}) %all-gather.4.cloned.1.call-update) | async-done | bytes 8388624 | tf_op jit(solution)/shard_map/all_gather | solution.py:56
  287.7 311.1 %all-gather.6.cloned.1.call-done = bf16[4096,1024]{1,0:T(8,128)(2,1)} async-done(((bf16[64,1024]{1,0:T(8,128)(2,1)}), bf16[4096,1024]{1,0:T(8,128)(2,1)}) %all-gather.6.cloned.1.call-update) | async-done | bytes 8388624 | tf_op jit(solution)/shard_map/all_gather | solution.py:57
  598.9 169.1 %while.18 = (s32[]{:T(128)}, f32[384,8]{0,1:T(8,128)S(1)}, f32[384,8]{0,1:T(8,128)S(1)}, f32[384,8,128]{0,2,1:T(8,128)}, s32[8]{0:T(128)S(1)}, /*index=5*/s32[64...) while((s32[]{:T(128)}, f32[384,8]{0,1:T(8,128)S(1)}, ...), condition=%wide.region_4.5_spmd.clone.clone, body=%wide.region_0.4_spmd.clone.clone.sunk | while | flops 975165952 | bytes 34383340 | solution.py:70
  598.9 0.6 dynamic_slice.35
  600.0 1.7 constant_dynamic-slice_fusion.3
  602.4 1.5 fusion.48
  603.8 5.3 fusion.49
  609.1 4.1 fusion.50
  613.7 5.8 bitcast_add_fusion.2
  619.6 0.6 dynamic_slice.35
  620.7 1.7 constant_dynamic-slice_fusion.3
  623.1 1.5 fusion.48
  624.5 5.3 fusion.49
  629.8 4.1 fusion.50
  634.5 6.2 bitcast_add_fusion.2
  640.7 0.6 dynamic_slice.35
  641.8 1.7 constant_dynamic-slice_fusion.3
  644.2 1.5 fusion.48
  645.7 5.3 fusion.49
  651.0 4.1 fusion.50
  655.6 6.3 bitcast_add_fusion.2
  661.9 0.6 dynamic_slice.35
  663.0 1.7 constant_dynamic-slice_fusion.3
  665.4 1.5 fusion.48
  666.9 5.3 fusion.49
  672.2 4.1 fusion.50
  676.8 6.3 bitcast_add_fusion.2
  683.1 0.6 dynamic_slice.35
  684.2 1.7 constant_dynamic-slice_fusion.3
  686.6 1.5 fusion.48
  688.1 5.3 fusion.49
  693.4 4.1 fusion.50
  698.0 6.3 bitcast_add_fusion.2
  704.3 0.6 dynamic_slice.35
  705.4 1.7 constant_dynamic-slice_fusion.3
  707.8 1.5 fusion.48
  709.3 5.3 fusion.49
  714.6 4.1 fusion.50
  719.2 6.3 bitcast_add_fusion.2
  725.5 0.6 dynamic_slice.35
  726.6 1.7 constant_dynamic-slice_fusion.3
  729.0 1.5 fusion.48
  730.5 5.3 fusion.49
  735.8 4.1 fusion.50
  740.4 6.3 bitcast_add_fusion.2
  747.8 1.7 constant_dynamic-slice_fusion.3
  750.2 1.5 fusion.48
  751.7 5.3 fusion.49
  757.0 4.1 fusion.50
  761.6 6.3 bitcast_add_fusion.2
  767.9 1.5 divide_convert_fusion
  769.5 138.6 %all-gather.8.cloned.1.call-done = bf16[1024,4096]{0,1:T(8,128)(2,1)} async-done(((bf16[1024,64]{0,1:T(8,128)(2,1)}), bf16[1024,4096]{0,1:T(8,128)(2,1)}) %all-gather.8.cloned.1.call-update) | async-done | bytes 8388624 | tf_op jit(solution)/shard_map/all_gather | solution.py:79
  908.0 9.6 fusion.25
  917.6 0.7 copy-done.2
  918.3 168.5 %all-reduce.2.cloned.1.call-done = f32[384,4096]{1,0:T(8,128)} async-done(((f32[384,4096]{1,0:T(8,128)}), f32[384,4096]{1,0:T(8,128)}) %all-reduce.2.cloned.1.call-update) | async-done | bytes 6291472 | tf_op jit(solution)/shard_map/psum | solution.py:83
  1086.8 2.6 add_convert_fusion
  (88 shorter events, 10.5 us)
Async XLA Ops:
  6.5 281.2 %all-gather.4.cloned.1.call-start = ((), (), s32[]{:S(2)}) async-start(), calls=%async_computation | async-start | bytes 8519680 | tf_op jit(solution)/shard_map/all_gather | solution.py:56
  7.3 591.6 %all-gather.6.cloned.1.call-start = ((), (), s32[]{:S(2)}) async-start(), calls=%async_computation.1 | async-start | bytes 8519680 | tf_op jit(solution)/shard_map/all_gather | solution.py:57
  8.0 900.0 %all-gather.8.cloned.1.call-start = ((), (), s32[]{:S(2)}) async-start(), calls=%async_computation.2 | async-start | bytes 8519680 | tf_op jit(solution)/shard_map/all_gather | solution.py:79
  8.7 1078.0 %all-reduce.2.cloned.1.call-start = ((), (), s32[]{:S(2)}) async-start(), calls=%async_computation.3 | async-start | bytes 12582912 | tf_op jit(solution)/shard_map/psum | solution.py:83
  598.9 3.4 copy-start.1
  619.6 3.4 copy-start.1
  640.7 3.4 copy-start.1
  661.9 3.4 copy-start.1
  683.1 3.4 copy-start.1
  704.3 3.4 copy-start.1
  725.5 3.4 copy-start.1
  746.7 3.4 copy-start.1
  917.6 0.7 copy-start.2
  917.6 169.2 %copy-start = (bf16[384,1024]{1,0:T(8,128)(2,1)S(1)}, bf16[384,1024]{1,0:T(8,128)(2,1)}, u32[]{:S(2)}) copy-start(bf16[384,1024]{1,0:T(8,128)(2,1)} %param.16) | copy-start | bytes 2359300
Sparse Core Ops, SparseCore 0:
  9.1 278.5 all-gather.3
  289.5 309.2 all-gather.5
  600.6 307.3 all-gather.7
  917.7 168.9 all-reduce.1
where the time goes:
time: 1100 us
  waiting for transfers between devices  894 us (81%)
  matrix products  113 us (10%)
  other arithmetic  39.4 us (4%)
  local copies, waits for them, and re-layouts  31.3 us (3%)
  between operations  13.2 us (1%)
    all_gather x1, waiting for transfers between devices, on_device(): lax.all_gather(values, 'wide', axis=0, tiled=True)  311 us
    all_gather x1, waiting for transfers between devices, on_device(): lax.all_gather(keys, 'wide', axis=0, tiled=True)  274 us
    psum x1, waiting for transfers between devices, on_device(): summed = lax.psum(partial_terms, 'head')  168 us
    all_gather x1, waiting for transfers between devices, on_device(): lax.all_gather(out_weight, 'wide', axis=1, tiled=True)  139 us
    dot_general x8, matrix products, attend_block(): jnp.einsum('rht,thd->rhd', weights.astype(jnp.bfloat16), value_block, pre...  49.7 us
    dot_general x8, matrix products, attend_block(): jnp.einsum('rhd,thd->rht', query_rows, key_block, preferred_element_type=...  42.1 us
    reduce_sum x8, other arithmetic, attend_block(): run_total = run_total * factor + jnp.sum(weights, axis=2)  32.7 us
  transfers between devices with their start and end apart: 4, of which 4 were waited for; matrix products, arithmetic and copies ran while one was open for 16% of the time, Pallas kernels for 0%

commit v1 on v0

v1 whole, which is shorter than its diff:
```python
import functools
import math

import jax
import jax.numpy as jnp
from jax import lax
from jax.experimental import pallas as pl
from jax.experimental.pallas import tpu as pltpu
from jax.sharding import Mesh, PartitionSpec as P

HSIZE = 128
TOKF = 64
MESH = pl.DeviceIdType.MESH
AXES = ("xl", "y", "z", "xh", "core")
NY, NZ = 4, 8
NG = 8
CHUNK = NG * TOKF
HIDDEN = -1e30
FLOOR = -1e29
LOG2E_SCALE = 1.0 / (math.log(2.0) * math.sqrt(HSIZE))
ROWS = 384
FEATS = 4096
COLS = 1024
A_FEATS = 2048
STREAM = 4


def _kernel(
    q_ref, k_ref, v_ref, bnd_ref, oh_ref, w_ref, res_ref, gate_ref, out_ref,
    k2, vbuf, vt, qbuf, bbuf, qt, m_sc, l_sc, acc, satt, att, wt, wsib,
    loc, ka_s, ka_r, va_s, va_r, q_s, q_r, b_s, b_r, kv_s, kv_r,
    w0_s, w0_r, wx_s, wx_r, wya_s, wya_r, wza_s, wza_r, wzb_s, wzb_r, wyb_s, wyb_r,
    at_s, at_r, sb_s, sb_r,
):
    xl, y, z = lax.axis_index("xl"), lax.axis_index("y"), lax.axis_index("z")
    xh, core = lax.axis_index("xh"), lax.axis_index("core")
    g = xl * NY + y
    head = xh * 2 + core
    ylo = lax.rem(y, 2)
    home = core == y // 2
    away = core != y // 2

    def group(off):
        p = lax.rem(g + off + NG, NG)
        return p, (p // NY, lax.rem(p, NY), z, xh, core)

    def across(off, other):
        p = lax.rem(g + off + NG, NG)
        return (p // NY, lax.rem(p, NY), z, 1 - xh if other else xh, core)

    def zpeer(d):
        return (xl, y, lax.rem(z + d + NZ, NZ), xh, core)

    def ypeer(d):
        return (xl, lax.rem(y + d + NY, NY), z, xh, core)

    sibling = (xl, y, z, xh, 1 - core)

    def remote(src, dst, s, r, dev):
        return pltpu.make_async_remote_copy(
            src_ref=src, dst_ref=dst, send_sem=s, recv_sem=r, device_id=dev, device_id_type=MESH
        )

    bar = pltpu.get_barrier_semaphore()
    for off in range(1, NG):
        pl.semaphore_signal(bar, 1, device_id=group(off)[1], device_id_type=MESH)
    for off in range(NG):
        pl.semaphore_signal(bar, 1, device_id=across(off, True), device_id_type=MESH)
    for d in (1, -1):
        pl.semaphore_signal(bar, 1, device_id=zpeer(d), device_id_type=MESH)
    pl.semaphore_signal(bar, 1, device_id=sibling, device_id_type=MESH)
    pl.semaphore_wait(bar, 18)

    def tok_rows(i):
        return pl.ds(pl.multiple_of(i * TOKF, TOKF), TOKF)

    def head_cols(i):
        return pl.ds(pl.multiple_of(i * HSIZE, HSIZE), HSIZE)

    def k_copy(s, p, dev, src_g):
        return remote(k_ref.at[:, head_cols(p)], k2.at[z, tok_rows(src_g), 0:HSIZE], ka_s.at[s], ka_r.at[s], dev)

    def v_copy(s, p, dev, src_g):
        return remote(v_ref.at[:, head_cols(p)], vbuf.at[z, tok_rows(src_g), :], va_s.at[s], va_r.at[s], dev)

    def q_copy(s, p, dev):
        return remote(q_ref.at[:, head_cols(p)], qbuf.at[7 - s], q_s.at[s], q_r.at[s], dev)

    def b_copy(s, dev):
        return remote(bnd_ref, bbuf.at[7 - s], b_s.at[s], b_r.at[s], dev)

    w0 = remote(w_ref, wsib, w0_s, w0_r, sibling)

    @pl.when(away)
    def _():
        w0.start()

    for s in range(1, NG):
        p, dev = group(s)
        k_copy(s, p, dev, g).start()
        v_copy(s, p, dev, g).start()
    k_own = pltpu.make_async_copy(k_ref.at[:, head_cols(g)], k2.at[z, tok_rows(g), 0:HSIZE], loc.at[0])
    v_own = pltpu.make_async_copy(v_ref.at[:, head_cols(g)], vbuf.at[z, tok_rows(g), :], loc.at[1])
    q_own = pltpu.make_async_copy(q_ref.at[:, head_cols(g)], qbuf.at[7], loc.at[2])
    k_own.start()
    v_own.start()
    q_own.start()
    for s in range(1, NG):
        p, dev = group(s)
        q_copy(s, p, dev).start()
        b_copy(s, dev).start()

    def fill(i, _):
        zi, bi = i // NG, lax.rem(i, NG)
        k2[zi, tok_rows(bi), HSIZE : 2 * HSIZE] = jnp.broadcast_to(
            oh_ref[pl.ds(i, 1), :], (TOKF, HSIZE)
        ).astype(jnp.bfloat16)
        return 0

    lax.fori_loop(0, NZ * NG, fill, 0)
    m_sc[...] = jnp.full(m_sc.shape, FLOOR, jnp.float32)
    l_sc[...] = jnp.zeros(l_sc.shape, jnp.float32)
    acc[...] = jnp.zeros(acc.shape, jnp.float32)
    qt[HSIZE : 2 * HSIZE, :] = jnp.zeros((HSIZE, NG * ROWS), jnp.bfloat16)
    bbuf[7] = bnd_ref[...]

    def feat_cols(h):
        return pl.ds(pl.multiple_of(h * COLS, COLS), COLS)

    def wx_copy(src, c, t):
        h = xh * 2 + c
        return remote(src, wt.at[ylo, z, :, feat_cols(h)], wx_s.at[c, t], wx_r.at[xh, c], (t, y, z, xl, core))

    def wx_self(src, c):
        h = xh * 2 + c
        return pltpu.make_async_copy(src, wt.at[ylo, z, :, feat_cols(h)], wx_r.at[xh, c])

    def wx_each(own, act):
        for t in range(2):
            is_self = jnp.logical_and(xl == xh, xl == t)
            for which in range(2):
                src = w_ref if which == 0 else wsib
                c = core if which == 0 else 1 - core

                @pl.when(jnp.logical_and(home, is_self))
                def _():
                    if own:
                        act(wx_self(src, c))

                @pl.when(jnp.logical_and(home, jnp.logical_not(is_self)))
                def _():
                    act(wx_copy(src, c, t))

    @pl.when(home)
    def _():
        w0.wait_recv()

    wx_each(True, lambda cp: cp.start())

    def kv_piece(slot, which):
        return k2.at[slot, :, 0:HSIZE] if which == 0 else vbuf.at[slot]

    def slot_of(d, r):
        return lax.rem(z - d * r + 2 * NZ, NZ)

    def ring_dirs(r, which):
        if r < 4:
            return (1, -1)
        return (1,) if which == 0 else (-1,)

    def kv_send(d, r, which):
        slot = slot_of(d, r - 1)
        ref = kv_piece(slot, which)
        i = 0 if d == 1 else 1
        return remote(ref, ref, kv_s.at[i, r, which], kv_r.at[i, r, which], zpeer(d))

    def kv_recv(d, r, which):
        slot = slot_of(d, r)
        ref = kv_piece(slot, which)
        i = 0 if d == 1 else 1
        return remote(ref, ref, kv_s.at[i, r, which], kv_r.at[i, r, which], zpeer(d))

    for which in range(2):
        for s in range(1, NG):
            src, _unused = group(-s)
            if which == 0:
                k_copy(s, 0, sibling, src).wait_recv()
            else:
                v_copy(s, 0, sibling, src).wait_recv()
        (k_own if which == 0 else v_own).wait()
        for d in ring_dirs(1, which):
            kv_send(d, 1, which).start()

    def wya_copy(lo, d):
        ref = wt.at[lo, z, :, 0:A_FEATS]
        return remote(ref, ref, wya_s.at[d], wya_r.at[lo], ypeer(d))

    def wza_half(slot, half):
        if half is None:
            return wt.at[:, slot, :, 0:A_FEATS]
        return wt.at[half, slot, :, 0:A_FEATS]

    def wzb_half(slot, half):
        if half is None:
            return wt.at[ylo, slot, :, A_FEATS:FEATS]
        return wt.at[ylo, slot, 32 * half : 32 * half + 32, A_FEATS:FEATS]

    def wz_copy(piece, s, r, d, rnd, sending):
        slot = slot_of(d, rnd - 1) if sending else slot_of(d, rnd)
        i = 0 if d == 1 else 1
        ref = piece(slot, None if rnd < 4 else i)
        return remote(ref, ref, s.at[i, rnd], r.at[i, rnd], zpeer(d))

    def wza(d, rnd, sending):
        return wz_copy(wza_half, wza_s, wza_r, d, rnd, sending)

    def wzb(d, rnd, sending):
        return wz_copy(wzb_half, wzb_s, wzb_r, d, rnd, sending)

    def wyb_copy(lo, slot, n, d):
        ref = wt.at[lo, slot, :, A_FEATS:FEATS]
        return remote(ref, ref, wyb_s.at[n, d], wyb_r.at[lo, n], ypeer(d))

    def nth_slot(n):
        return lax.rem(z + (0, -1, 1, -2, 2, -3, 3, 4)[n] + NZ, NZ)

    @pl.when(home)
    def _():
        for xs in range(2):
            for c in range(2):
                ref = wt.at[ylo, z, :, feat_cols(xs * 2 + c)]
                pltpu.make_async_copy(ref, ref, wx_r.at[xs, c]).wait()
        for d in (1, 3, 2):
            wya_copy(ylo, d).start()
        for d in (1, -1):
            wzb(d, 1, True).start()
        for d in (1, 3, 2):
            wyb_copy(ylo, nth_slot(0), 0, d).start()

    def queries_in(p):
        cols = slice(p * ROWS, (p + 1) * ROWS)
        qt[0:HSIZE, cols] = qbuf[p].T
        frame = lax.broadcasted_iota(jnp.int32, (TOKF, ROWS), 0).astype(jnp.float32)
        qt[HSIZE : HSIZE + TOKF, cols] = jnp.where(frame < bbuf[p, 0:1, :], 0.0, HIDDEN).astype(
            jnp.bfloat16
        )

    def vt_cols(slot):
        return pl.ds(pl.multiple_of(slot * CHUNK, CHUNK), CHUNK)

    for s in range(7, 0, -1):
        q_copy(s, 0, sibling).wait_recv()
        b_copy(s, sibling).wait_recv()
        queries_in(7 - s)
    q_own.wait()
    queries_in(7)

    wide = slice(0, STREAM * ROWS)

    def stream(slot):
        vt[:, vt_cols(slot)] = vbuf[slot].T
        s = jnp.dot(k2[slot], qt[:, wide], preferred_element_type=jnp.float32)
        m_old = m_sc[0:1, :]
        m_new = jnp.maximum(m_old, jnp.max(s, axis=0, keepdims=True))
        p = jnp.exp2((s - m_new) * LOG2E_SCALE)
        shrink = jnp.exp2((m_old - m_new) * LOG2E_SCALE)
        m_sc[0:1, :] = m_new
        l_sc[0:1, :] = l_sc[0:1, :] * shrink + jnp.sum(p, axis=0, keepdims=True)
        acc[...] = acc[...] * shrink + jnp.dot(
            vt[:, vt_cols(slot)], p.astype(jnp.bfloat16), preferred_element_type=jnp.float32
        )

    def attend(n):
        stream(nth_slot(n))

    attend(0)
    for rnd in range(1, 5):
        for which in range(2):
            for d in ring_dirs(rnd, which):
                kv_recv(d, rnd, which).wait_recv()
            if rnd < 4:
                for d in ring_dirs(rnd + 1, which):
                    kv_send(d, rnd + 1, which).start()

        @pl.when(home)
        def _():
            for i, d in enumerate((1, -1)):
                wzb(d, rnd, False).wait_recv()
                if rnd < 4:
                    wzb(d, rnd + 1, True).start()
                    n = 2 * rnd - 1 + i
                    for e in (1, 3, 2):
                        wyb_copy(ylo, nth_slot(n), n, e).start()
            if rnd == 4:
                for e in (1, 3, 2):
                    wyb_copy(ylo, nth_slot(7), 7, e).start()

        if rnd == 2:
            for lo in range(2):

                @pl.when(y != core * 2 + lo)
                def _():
                    wya_copy(lo, 1).wait_recv()

            for d in (1, -1):
                wza(d, 1, True).start()
        attend(2 * rnd - 1)
        if rnd < 4:
            attend(2 * rnd)

    def att_rows(h, p):
        return pl.ds(pl.multiple_of((h * NG + p) * HSIZE, HSIZE), HSIZE)

    def att_copy(off, other, h, src_g):
        i = 1 if other else 0
        return remote(
            satt.at[(off + 7) % 8], att.at[att_rows(h, src_g), :], at_s.at[i, off], at_r.at[i, off], across(off, other)
        )

    att_own = pltpu.make_async_copy(satt.at[7], att.at[att_rows(head, g), :], loc.at[3])

    def give(p):
        off = (p + 1) % 8
        att_copy(off, True, head, g).start()
        if off == 0:
            att_own.start()
        else:
            att_copy(off, False, head, g).start()

    def normed(p, mixed, total):
        empty = (bbuf[p, 0:1, :] == 0.0).astype(jnp.float32)
        satt[p] = (mixed / (total + empty)).astype(jnp.bfloat16)

    for p in range(STREAM):
        cols = slice(p * ROWS, (p + 1) * ROWS)
        normed(p, acc[:, cols], l_sc[0:1, cols])
        give(p)

    def wza_step(rnd):
        for d in (1, -1):
            wza(d, rnd, False).wait_recv()
            if rnd < 4:
                wza(d, rnd + 1, True).start()

    for p in range(STREAM, NG):
        s = jnp.dot(
            k2[...].reshape(NZ * CHUNK, 2 * HSIZE),
            qt[:, p * ROWS : (p + 1) * ROWS],
            preferred_element_type=jnp.float32,
        )
        m_all = jnp.maximum(jnp.max(s, axis=0, keepdims=True), FLOOR)
        w = jnp.exp2((s - m_all) * LOG2E_SCALE)
        total = jnp.sum(w, axis=0, keepdims=True)
        mixed = jnp.dot(vt[...], w.astype(jnp.bfloat16), preferred_element_type=jnp.float32)
        normed(p, mixed, total)
        give(p)
        if p == STREAM + 1:
            wza_step(1)
        if p == STREAM + 3:
            wza_step(2)

    def sib_copy(off, other, mine):
        i = 1 if other else 0
        xs = 1 - xh if other else xh
        c = core if mine else 1 - core
        ref = att.at[att_rows(xs * 2 + c, lax.rem(g - off + NG, NG)), :]
        return remote(ref, ref, sb_s.at[i, off], sb_r.at[i, off], sibling)

    for off in (1, 2, 3, 4, 5, 6, 7, 0):
        for other in (False, True):
            if off == 0 and not other:
                att_own.wait()
            else:
                xs = 1 - xh if other else xh
                att_copy(off, other, xs * 2 + core, lax.rem(g - off + NG, NG)).wait_recv()
            sib_copy(off, other, True).start()
    wza_step(3)
    for off in range(NG):
        for other in (False, True):
            sib_copy(off, other, False).wait_recv()
    wza_step(4)
    for lo in range(2):

        @pl.when(y != core * 2 + lo)
        def _():
            for n in range(8):
                wyb_copy(lo, nth_slot(n), n, 1).wait_recv()

    def project(i, _):
        lo, half = i // 2, lax.rem(i, 2)
        w = wt[lo, pl.ds(half * 4, 4)].reshape(256, FEATS)
        part = jnp.dot(w, att[...], preferred_element_type=jnp.float32)
        cols = pl.ds(pl.multiple_of(i * 256, 256), 256)
        out_ref[:, cols] = (
            res_ref[:, cols].astype(jnp.float32) + jnp.tanh(gate_ref[:, cols]) * part.T
        ).astype(out_ref.dtype)
        return 0

    lax.fori_loop(0, 4, project, 0)

    @pl.when(away)
    def _():
        w0.wait_send()

    for t in range(2):
        for which in range(2):
            src = w_ref if which == 0 else wsib
            c = core if which == 0 else 1 - core

            @pl.when(jnp.logical_and(home, jnp.logical_not(jnp.logical_and(xl == xh, xl == t))))
            def _():
                wx_copy(src, c, t).wait_send()

    for s in range(1, NG):
        p, dev = group(s)
        k_copy(s, p, dev, g).wait_send()
        v_copy(s, p, dev, g).wait_send()
        q_copy(s, p, dev).wait_send()
        b_copy(s, dev).wait_send()
    for rnd in range(1, 5):
        for which in range(2):
            for d in ring_dirs(rnd, which):
                kv_send(d, rnd, which).wait_send()
        for d in (1, -1):
            wza(d, rnd, True).wait_send()

    @pl.when(home)
    def _():
        for d in (1, 3, 2):
            wya_copy(ylo, d).wait_send()
        for rnd in range(1, 5):
            for d in (1, -1):
                wzb(d, rnd, True).wait_send()
        for n in range(8):
            for d in (1, 3, 2):
                wyb_copy(ylo, nth_slot(n), n, d).wait_send()

    for off in range(NG):
        for other in (False, True):
            if other or off:
                att_copy(off, other, head, g).wait_send()
            sib_copy(off, other, True).wait_send()


def _on_device(queries, keys, values, frame_mask, frame_slot, out_weight, residual, gate):
    seen = jnp.sum(frame_mask, axis=1).astype(jnp.float32)
    bounds = jnp.broadcast_to(seen[None, :], (8, ROWS))
    order = frame_slot.reshape(NG, NZ).T.reshape(NG * NZ)
    onehot = (order[:, None] == jnp.arange(HSIZE, dtype=jnp.int32)[None, :]).astype(jnp.float32)
    dma = pltpu.SemaphoreType.DMA
    vmem = pl.BlockSpec(memory_space=pltpu.VMEM)
    hbm = pl.BlockSpec(memory_space=pl.ANY)
    bf16, f32 = jnp.bfloat16, jnp.float32
    return pl.pallas_call(
        _kernel,
        out_shape=jax.ShapeDtypeStruct((ROWS, COLS), bf16),
        in_specs=[hbm, hbm, hbm, vmem, vmem, vmem, vmem, vmem],
        out_specs=vmem,
        scratch_shapes=[
            pltpu.VMEM((NZ, CHUNK, 2 * HSIZE), bf16),
            pltpu.VMEM((NZ, CHUNK, HSIZE), bf16),
            pltpu.VMEM((HSIZE, NZ * CHUNK), bf16),
            pltpu.VMEM((NG, ROWS, HSIZE), bf16),
            pltpu.VMEM((NG, 8, ROWS), f32),
            pltpu.VMEM((2 * HSIZE, NG * ROWS), bf16),
            pltpu.VMEM((8, STREAM * ROWS), f32),
            pltpu.VMEM((8, STREAM * ROWS), f32),
            pltpu.VMEM((HSIZE, STREAM * ROWS), f32),
            pltpu.VMEM((NG, HSIZE, ROWS), bf16),
            pltpu.VMEM((FEATS, ROWS), bf16),
            pltpu.VMEM((2, NZ, TOKF, FEATS), bf16),
            pltpu.VMEM((TOKF, COLS), bf16),
            dma((4,)),
            dma((8,)), dma((8,)), dma((8,)), dma((8,)),
            dma((8,)), dma((8,)), dma((8,)), dma((8,)),
            dma((2, 5, 2)), dma((2, 5, 2)),
            dma, dma,
            dma((2, 2)), dma((2, 2)),
            dma((4,)), dma((2,)),
            dma((2, 5)), dma((2, 5)),
            dma((2, 5)), dma((2, 5)),
            dma((8, 4)), dma((2, 8)),
            dma((2, 8)), dma((2, 8)),
            dma((2, 8)), dma((2, 8)),
        ],
        compiler_params=pltpu.CompilerParams(
            collective_id=0, has_side_effects=True, vmem_limit_bytes=58 * 2**20
        ),
    )(queries, keys, values, bounds, onehot, out_weight.T, residual, gate.reshape(1, COLS))


def solution(mesh):
    fine = Mesh(mesh.devices.reshape(2, NY, NZ, 2, 2), AXES)
    wide, head = ("xl", "y", "z"), ("xh", "core")
    return jax.shard_map(
        _on_device,
        mesh=fine,
        in_specs=(
            P(wide, head),
            P(wide, head),
            P(wide, head),
            P(wide, None),
            P(),
            P(head, wide),
            P(wide, head),
            P(head),
        ),
        out_specs=P(wide, head),
        check_vma=False,
    )
```

time: 1100 us -> 122 us (0.11)
  waiting for transfers between devices: 894 us -> 0 us
  Pallas kernels: 0 us -> 117 us
  matrix products: 113 us -> 0 us
  other arithmetic: 39.4 us -> 1.61 us
  local copies, waits for them, and re-layouts: 31.3 us -> 3.54 us
  between operations: 13.2 us -> 0.02 us
    all_gather x3 -> x0, waiting for transfers between devices: 723 us -> none  [the longest x1 311 us: on_device(): lax.all_gather(values, 'wide', axis=0, tiled=True)]
    psum x1 -> x0, waiting for transfers between devices: 168 us -> none  [on_device(): summed = lax.psum(partial_terms, 'head')]
    pallas_call x0 -> x1, Pallas kernels: none -> 117 us  [_on_device(): pl.pallas_call(_kernel, out_shape=jax.ShapeDtypeStruct((ROWS, COLS), bf16...]
    dot_general x25 -> x0, matrix products: 113 us -> none  [the longest x8 49.7 us: attend_block(): jnp.einsum('rht,thd->rhd', weights.astype(jnp.bfloat16), value_block, pre...]
    reduce_sum x17 -> x1, other arithmetic: 34.4 us -> 0.92 us  [_on_device(): seen = jnp.sum(frame_mask, axis=1).astype(jnp.float32)]
    dynamic_slice x32 -> x0, local copies, waits for them, and re-layouts: 26.9 us -> none  [the longest x16 18.1 us: inner(): value_rows = lax.dynamic_slice_in_dim(all_values, offset, block_size, 0)]
  transfers between devices with their start and end apart: 4 -> 0, of which waited for: 4 -> 0; matrix products, arithmetic and copies ran while one was open for 16% -> 0% of each run, Pallas kernels for 0% -> 0%
where the time goes in v1:
time: 122 us
  Pallas kernels  117 us (96%)
  local copies, waits for them, and re-layouts  3.54 us (3%)
  other arithmetic  1.61 us (1%)
    pallas_call x1, Pallas kernels, _on_device(): pl.pallas_call(_kernel, out_shape=jax.ShapeDtypeStruct((ROWS, COLS), bf16...  117 us
    unnamed x3, local copies, waits for them, and re-layouts  2.71 us

profile of v1, /device:TPU:1, one launch (start us, length us, event | category | flops | bytes accessed | tf_op | source)
XLA Modules:
  0.0 122.1 jit_solution(4813428042881328258)
XLA Ops:
  0.0 0.9 reduce_sum.9
  0.9 0.0 copy-start
  0.9 0.6 copy-done
  1.6 0.1 reshape.10
  1.7 0.1 copy.9
  1.7 0.1 eq.15
  1.8 0.6 broadcast_in_dim.2.bnd_ref
  2.4 0.7 fusion.oh_ref
  3.1 116.9 %shard_map.82 = bf16[384,1024]{1,0:T(8,128)(2,1)} custom-call(bf16[384,1024]{1,0:T(8,128)(2,1)} %q_ref.1, bf16[64,1024]{1,0:T(8,128)(2,1)} %k_ref.1, bf16[64,1024]{1,0:T(8,128)(2,1)} %v_ref.1, f32[8,384]{1,0:T(8,128)} %broadcast_in_dim.2.bnd_ref, f32[64,128]{1,0:T(8,128)} %fusion.oh_ref, bf16[64,1024]{1,0:T(8,128)(2,1)} %bitcast.3, ...), custom_call_target="tpu_custom_call" | custom-call | tf_op jit(solution)/shard_map/pallas_call | solution.py:454
  120.1 2.1 %copy.11 = bf16[384,1024]{1,0:T(8,128)(2,1)} copy(bf16[384,1024]{1,0:T(8,128)(2,1)} %shard_map.82) | data formatting | bytes 1572864
  (1 shorter events, 0.0 us)
Async XLA Ops:
  0.9 0.7 copy-start

commit v2 on v0

v2 whole, which is shorter than its diff:
```python
import functools
import math

import jax
import jax.numpy as jnp
from jax import lax
from jax.experimental import pallas as pl
from jax.experimental.pallas import tpu as pltpu
from jax.sharding import Mesh, PartitionSpec as P

HSIZE = 128
TOKF = 64
MESH = pl.DeviceIdType.MESH
AXES = ("xl", "y", "z", "xh", "core")
NY, NZ = 4, 8
NG = 8
CHUNK = NG * TOKF
HIDDEN = -1e30
FLOOR = -1e29
LOG2E_SCALE = 1.0 / (math.log(2.0) * math.sqrt(HSIZE))
ROWS = 384
FEATS = 4096
COLS = 1024
OWN = 512
STREAM = 4
ORDER = (0, 2, 1, 3)
PLACE = {(dy, o): 2 * i + o for i, dy in enumerate(ORDER) for o in range(2)}
PLANE = tuple((dy, o) for dy in ORDER for o in range(2) if (dy, o) != (0, 0))


def _kernel(
    q_ref, k_ref, v_ref, mask_ref, slot_ref, w_ref, res_ref, gate_ref, out_ref,
    k2, vbuf, vt, qbuf, bnd, bbuf, qt, m_sc, l_sc, acc, satt, att, wt, wown, res, res2, upd,
    loc, ka_s, ka_r, va_s, va_r, q_s, q_r, b_s, b_r, kv_s, kv_r,
    wx_s, wx_r, wr_s, wr_r, wy_s, wy_r, rl_s,
    t1_s, t1_r, t2_s, t2_r, t3_s, t3_r, sb_s, sb_r, rs_s, rs_r, up_s, up_r,
):
    xl, y, z = lax.axis_index("xl"), lax.axis_index("y"), lax.axis_index("z")
    xh, core = lax.axis_index("xh"), lax.axis_index("core")
    g = xl * NY + y
    head = xh * 2 + core
    ylo = lax.rem(y, 2)
    home = jnp.logical_and(core == y // 2, xl == ylo)

    def ypos(d):
        return lax.rem(y + d + NY, NY)

    def zpos(d):
        return lax.rem(z + d + NZ, NZ)

    def dev(other_xl=0, dy=0, dz=0, other_xh=0, other_core=0):
        return (
            1 - xl if other_xl else xl,
            ypos(dy),
            zpos(dz),
            1 - xh if other_xh else xh,
            1 - core if other_core else core,
        )

    def remote(src, dst, s, r, to):
        return pltpu.make_async_remote_copy(
            src_ref=src, dst_ref=dst, send_sem=s, recv_sem=r, device_id=to, device_id_type=MESH
        )

    sibling = dev(other_core=1)

    bar = pltpu.get_barrier_semaphore()
    peers = [dev(other_xl=o, dy=dy) for dy, o in PLANE]
    peers += [dev(dz=1), dev(dz=-1), sibling]
    peers += [dev(other_xl=o, other_xh=1) for o in (0, 1)]
    peers += [dev(other_xl=o, other_xh=h, other_core=1) for o, h in ((0, 1), (1, 0), (1, 1))]
    for to in peers:
        pl.semaphore_signal(bar, 1, device_id=to, device_id_type=MESH)

    def own_copy(src, dst, i):
        return pltpu.make_async_copy(src, dst, loc.at[i])

    wown[...] = w_ref[...].T
    ones = jnp.ones((8, mask_ref.shape[1]), jnp.bfloat16)
    bnd[...] = lax.dot_general(
        ones, mask_ref[...].astype(jnp.bfloat16), (((1,), (1,)), ((), ())), preferred_element_type=jnp.float32
    )
    bbuf[PLACE[(0, 0)]] = bnd[...]
    pl.semaphore_wait(bar, len(peers))

    def feat_cols(h):
        return pl.ds(pl.multiple_of(h * COLS, COLS), COLS)

    wx_copy = remote(wown, wt.at[z, :, feat_cols(head)], wx_s, wx_r.at[head], (ylo, y, z, xl, y // 2))
    wx_own = pltpu.make_async_copy(wown, wt.at[z, :, feat_cols(head)], wx_r.at[head])
    wx_is_self = jnp.logical_and(home, xl == xh)

    def tok_rows(i):
        return pl.ds(pl.multiple_of(i * TOKF, TOKF), TOKF)

    def head_cols(i):
        return pl.ds(pl.multiple_of(i * HSIZE, HSIZE), HSIZE)

    def group(dy, o):
        return (1 - xl if o else xl) * NY + ypos(dy)

    def k_copy(i, dy, o, src_g):
        return remote(
            k_ref.at[:, head_cols(group(dy, o))], k2.at[z, tok_rows(src_g), 0:HSIZE],
            ka_s.at[i], ka_r.at[i], dev(other_xl=o, dy=dy),
        )

    def v_copy(i, dy, o, src_g):
        return remote(
            v_ref.at[:, head_cols(group(dy, o))], vbuf.at[z, tok_rows(src_g), :],
            va_s.at[i], va_r.at[i], dev(other_xl=o, dy=dy),
        )

    def q_copy(i, dy, o):
        return remote(
            q_ref.at[:, head_cols(group(dy, o))], qbuf.at[PLACE[(-dy % NY, o)]],
            q_s.at[i], q_r.at[i], dev(other_xl=o, dy=dy),
        )

    def b_copy(i, dy, o):
        return remote(bnd, bbuf.at[PLACE[(-dy % NY, o)]], b_s.at[i], b_r.at[i], dev(other_xl=o, dy=dy))

    def window(i):
        return pl.ds(pl.multiple_of(i * OWN, OWN), OWN)

    k_own = own_copy(k_ref.at[:, head_cols(g)], k2.at[z, tok_rows(g), 0:HSIZE], 0)
    v_own = own_copy(v_ref.at[:, head_cols(g)], vbuf.at[z, tok_rows(g), :], 1)
    q_own = own_copy(q_ref.at[:, head_cols(g)], qbuf.at[PLACE[(0, 0)]], 2)
    res_in = own_copy(res_ref.at[:, window(xl)], res, 3)
    partner = dev(other_xl=1)
    res_out = remote(res_ref.at[:, window(1 - xl)], res2, rs_s, rs_r, partner)
    for i, (dy, o) in enumerate(PLANE):
        k_copy(i, dy, o, g).start()
    for i, (dy, o) in enumerate(PLANE):
        v_copy(i, dy, o, g).start()
    k_own.start()
    v_own.start()

    @pl.when(wx_is_self)
    def _():
        wx_own.start()

    @pl.when(jnp.logical_not(wx_is_self))
    def _():
        wx_copy.start()

    for i, (dy, o) in enumerate(PLANE):
        q_copy(i, dy, o).start()
        b_copy(i, dy, o).start()
    q_own.start()
    res_in.start()
    res_out.start()

    lane = lax.broadcasted_iota(jnp.int32, (TOKF, HSIZE), 1)

    def fill(i, _):
        zi, bi = i // NG, lax.rem(i, NG)
        k2[zi, tok_rows(bi), HSIZE : 2 * HSIZE] = jnp.where(lane == slot_ref[bi * NZ + zi], 1.0, 0.0).astype(
            jnp.bfloat16
        )
        return 0

    lax.fori_loop(0, NZ * NG, fill, 0)
    m_sc[...] = jnp.full(m_sc.shape, FLOOR, jnp.float32)
    l_sc[...] = jnp.zeros(l_sc.shape, jnp.float32)
    acc[...] = jnp.zeros(acc.shape, jnp.float32)
    qt[HSIZE : 2 * HSIZE, :] = jnp.zeros((HSIZE, NG * ROWS), jnp.bfloat16)

    def ring_dirs(r, which):
        if r < 4:
            return (1, -1)
        return (1,) if which == 0 else (-1,)

    class Ring:
        def __init__(self, piece, s, r):
            self.piece, self.s, self.r = piece, s, r

        def copy(self, d, r, which, steps):
            ref = self.piece(lax.rem(z - d * steps + 2 * NZ, NZ), which)
            i = 0 if d == 1 else 1
            return remote(ref, ref, self.s.at[i, r, which], self.r.at[i, r, which], dev(dz=d))

        def send(self, d, r, which):
            return self.copy(d, r, which, r - 1)

        def begin(self, which):
            for d in ring_dirs(1, which):
                self.send(d, 1, which).start()

        def step(self, r, pieces=(0, 1)):
            for which in pieces:
                for d in ring_dirs(r, which):
                    self.copy(d, r, which, r).wait_recv()
                    if r < 4 and d in ring_dirs(r + 1, which):
                        self.send(d, r + 1, which).start()

        def end(self):
            for r in range(1, 5):
                for which in range(2):
                    for d in ring_dirs(r, which):
                        self.send(d, r, which).wait_send()

    def half(which):
        return slice(32 * which, 32 * which + 32)

    kv_ring = Ring(lambda slot, w: vbuf.at[slot] if w else k2.at[slot, :, 0:HSIZE], kv_s, kv_r)
    w_ring = Ring(lambda slot, w: wt.at[slot, half(w)], wr_s, wr_r)

    def wy_copy(which, d, s):
        ref = wt.at[z, half(which)]
        return remote(ref, ref, s, wy_r.at[which], dev(dy=d))

    def wy_send(which, i):
        return wy_copy(which, (1, -1)[i], wy_s.at[which, i])

    place = lax.rem(y - 2 * core - xl + 2 * NY, NY)

    def relay_copy(which):
        return wy_copy(which, (1, -1)[which], rl_s)

    def relay():
        for which in range(2):

            @pl.when(place == (1, 3)[which])
            def _():
                wy_copy(which, 1, rl_s).wait_recv()
                relay_copy(which).start()

    def relayed():
        for which in range(2):

            @pl.when(jnp.logical_or(place == 2, place == (3, 1)[which]))
            def _():
                wy_copy(which, 1, rl_s).wait_recv()

    for i, (dy, o) in enumerate(PLANE):
        k_copy(i, dy, o, group(-dy, o)).wait_recv()
    k_own.wait()
    kv_ring.begin(0)
    for i, (dy, o) in enumerate(PLANE):
        v_copy(i, dy, o, group(-dy, o)).wait_recv()
    v_own.wait()
    kv_ring.begin(1)

    @pl.when(home)
    def _():
        for h in range(4):
            ref = wt.at[z, :, feat_cols(h)]
            pltpu.make_async_copy(ref, ref, wx_r.at[h]).wait()
        for which in range(2):
            for i in range(2):
                wy_send(which, i).start()

    kv_ring.step(1)
    relay()

    def queries_in(p):
        cols = slice(p * ROWS, (p + 1) * ROWS)
        qt[0:HSIZE, cols] = qbuf[p].T
        frame = lax.broadcasted_iota(jnp.int32, (TOKF, ROWS), 0).astype(jnp.float32)
        qt[HSIZE : HSIZE + TOKF, cols] = jnp.where(frame < bbuf[p, 0:1, :], 0.0, HIDDEN).astype(
            jnp.bfloat16
        )

    for i, (dy, o) in enumerate(PLANE):
        q_copy(i, dy, o).wait_recv()
        b_copy(i, dy, o).wait_recv()
        queries_in(PLACE[(-dy % NY, o)])
    q_own.wait()
    queries_in(PLACE[(0, 0)])

    def vt_cols(slot):
        return pl.ds(pl.multiple_of(slot * CHUNK, CHUNK), CHUNK)

    def attend(n):
        slot = zpos((0, -1, 1, -2, 2, -3, 3, 4)[n])
        vt[:, vt_cols(slot)] = vbuf[slot].T
        s = jnp.dot(k2[slot], qt[:, 0 : STREAM * ROWS], preferred_element_type=jnp.float32)
        m_old = m_sc[0:1, :]
        m_new = jnp.maximum(m_old, jnp.max(s, axis=0, keepdims=True))
        p = jnp.exp2((s - m_new) * LOG2E_SCALE)
        shrink = jnp.exp2((m_old - m_new) * LOG2E_SCALE)
        m_sc[0:1, :] = m_new
        l_sc[0:1, :] = l_sc[0:1, :] * shrink + jnp.sum(p, axis=0, keepdims=True)
        acc[...] = acc[...] * shrink + jnp.dot(
            vt[:, vt_cols(slot)], p.astype(jnp.bfloat16), preferred_element_type=jnp.float32
        )

    def head_slot(other_xl, other_xh, dy, other_core=0, part=None):
        h = (1 - xh if other_xh else xh) * 2 + (1 - core if other_core else core)
        p = h * NG + (1 - xl if other_xl else xl) * NY + ypos(-dy)
        if part is None:
            return att.at[pl.ds(pl.multiple_of(p * HSIZE, HSIZE), HSIZE), :]
        return att.at[pl.ds(pl.multiple_of(p * HSIZE + part * 64, 64), 64), :]

    def t1_copy(dy):
        return remote(satt.at[dy], head_slot(0, 0, 0), t1_s.at[dy], t1_r.at[dy], dev(dy=dy))

    def t1_got(dy):
        return remote(satt.at[dy], head_slot(0, 0, dy), t1_s.at[dy], t1_r.at[dy], sibling)

    def t2_copy(dy, h):
        src = head_slot(0, 0, dy) if dy else satt.at[0]
        return remote(src, head_slot(0, 0, dy), t2_s.at[dy, h], t2_r.at[dy, h], dev(other_xl=1, other_xh=h))

    def t2_got(dy, h):
        ref = head_slot(1, h, dy)
        return remote(ref, ref, t2_s.at[dy, h], t2_r.at[dy, h], sibling)

    def t3_copy(dy, h):
        ref = head_slot(1, h, dy, part=h)
        return remote(ref, ref, t3_s.at[dy, h], t3_r.at[dy, h], dev(other_xl=1, other_xh=1 - h))

    def t3_got(dy, h):
        ref = head_slot(0, 1, dy, part=h)
        return remote(ref, ref, t3_s.at[dy, h], t3_r.at[dy, h], sibling)

    def sb_copy(dy, o, h):
        ref = head_slot(o, h, dy)
        return remote(ref, ref, sb_s.at[dy, o, h], sb_r.at[dy, o, h], sibling)

    def sb_got(dy, o, h):
        ref = head_slot(o, h, dy, 1)
        return remote(ref, ref, sb_s.at[dy, o, h], sb_r.at[dy, o, h], sibling)

    att_own = own_copy(satt.at[0], head_slot(0, 0, 0), 4)

    def give(dy):
        if dy:
            t1_copy(dy).start()
        else:
            for h in range(2):
                t2_copy(0, h).start()
            att_own.start()

    def pass_on(dy):
        if dy:
            t1_got(dy).wait_recv()
            for h in range(2):
                t2_copy(dy, h).start()
        else:
            att_own.wait()
        sb_copy(dy, 0, 0).start()

    def take(dy):
        for h in range(2):
            t2_got(dy, h).wait_recv()
            t3_copy(dy, h).start()
            sb_copy(dy, 1, h).start()

    def take_far(dy):
        for h in range(2):
            t3_got(dy, h).wait_recv()
        sb_copy(dy, 0, 1).start()

    def normed(p, mixed, total):
        dy, o = ORDER[p // 2], p % 2
        empty = (bbuf[p, 0:1, :] == 0.0).astype(jnp.float32)
        cols = pl.ds(pl.multiple_of((1 - xl if o else xl) * ROWS, ROWS), ROWS)
        satt[dy, :, cols] = (mixed / (total + empty)).astype(jnp.bfloat16)

    def attend_block(p):
        s = jnp.dot(
            k2[...].reshape(NZ * CHUNK, 2 * HSIZE),
            qt[:, p * ROWS : (p + 1) * ROWS],
            preferred_element_type=jnp.float32,
        )
        m_all = jnp.maximum(jnp.max(s, axis=0, keepdims=True), FLOOR)
        w = jnp.exp2((s - m_all) * LOG2E_SCALE)
        total = jnp.sum(w, axis=0, keepdims=True)
        mixed = jnp.dot(vt[...], w.astype(jnp.bfloat16), preferred_element_type=jnp.float32)
        normed(p, mixed, total)

    attend(0)
    kv_ring.step(2)
    attend(1)
    attend(2)
    relayed()
    kv_ring.step(3)
    for which in range(2):
        w_ring.begin(which)
    attend(3)
    attend(4)
    kv_ring.step(4)
    attend(5)
    attend(6)
    attend(7)
    for p in range(STREAM):
        cols = slice(p * ROWS, (p + 1) * ROWS)
        normed(p, acc[:, cols], l_sc[0:1, cols])
        if p % 2:
            give(ORDER[p // 2])
    w_ring.step(1, (0,))
    attend_block(4)
    pass_on(ORDER[0])
    w_ring.step(1, (1,))
    attend_block(5)
    give(ORDER[2])
    pass_on(ORDER[1])
    take(ORDER[0])
    w_ring.step(2, (0,))
    attend_block(6)
    pass_on(ORDER[2])
    take(ORDER[1])
    w_ring.step(2, (1,))
    attend_block(7)
    give(ORDER[3])
    take_far(ORDER[0])
    w_ring.step(3, (0,))
    take(ORDER[2])
    pass_on(ORDER[3])
    take_far(ORDER[1])
    w_ring.step(3, (1,))
    take(ORDER[3])
    take_far(ORDER[2])
    take_far(ORDER[3])
    w_ring.step(4)
    for dy in ORDER:
        for o in range(2):
            for h in range(2):
                sb_got(dy, o, h).wait_recv()
    res_in.wait()
    res_out.wait_recv()

    def project(i, side, before, put):
        w = wt[4 * i : 4 * i + 4].reshape(256, FEATS)
        rows = pl.ds(pl.multiple_of(side * ROWS, ROWS), ROWS)
        summed = jnp.dot(w, att[:, rows], preferred_element_type=jnp.float32)
        scale = jnp.tanh(gate_ref[:, pl.ds(pl.multiple_of(xl * OWN + i * 256, 256), 256)])
        put((before.astype(jnp.float32) + scale * summed.T).astype(jnp.bfloat16))

    def up_copy(i):
        cols = pl.ds(pl.multiple_of(xl * OWN + i * 256, 256), 256)
        return remote(upd.at[i], out_ref.at[:, cols], up_s.at[i], up_r.at[i], partner)

    def up_got(i):
        cols = pl.ds(pl.multiple_of((1 - xl) * OWN + i * 256, 256), 256)
        return remote(upd.at[i], out_ref.at[:, cols], up_s.at[i], up_r.at[i], partner)

    for i in range(2):

        def put_far(x):
            upd[i] = x

        project(i, 1 - xl, res2[:, 256 * i : 256 * i + 256], put_far)
        up_copy(i).start()
    for i in range(2):

        def put_own(x):
            out_ref[:, pl.ds(pl.multiple_of(xl * OWN + i * 256, 256), 256)] = x

        project(i, xl, res[:, 256 * i : 256 * i + 256], put_own)
    for i in range(2):
        up_got(i).wait_recv()

    @pl.when(jnp.logical_not(wx_is_self))
    def _():
        wx_copy.wait_send()

    for i, (dy, o) in enumerate(PLANE):
        k_copy(i, dy, o, g).wait_send()
        v_copy(i, dy, o, g).wait_send()
        q_copy(i, dy, o).wait_send()
        b_copy(i, dy, o).wait_send()
    res_out.wait_send()
    kv_ring.end()

    w_ring.end()

    @pl.when(home)
    def _():
        for which in range(2):
            for i in range(2):
                wy_send(which, i).wait_send()

    for which in range(2):

        @pl.when(place == (1, 3)[which])
        def _():
            relay_copy(which).wait_send()

    for dy in ORDER:
        if dy:
            t1_copy(dy).wait_send()
        for h in range(2):
            t2_copy(dy, h).wait_send()
            t3_copy(dy, h).wait_send()
            for o in range(2):
                sb_copy(dy, o, h).wait_send()
    for i in range(2):
        up_copy(i).wait_send()


def _on_device(queries, keys, values, frame_mask, frame_slot, out_weight, residual, gate):
    dma = pltpu.SemaphoreType.DMA
    vmem = pl.BlockSpec(memory_space=pltpu.VMEM)
    hbm = pl.BlockSpec(memory_space=pl.ANY)
    smem = pl.BlockSpec(memory_space=pltpu.SMEM)
    bf16, f32 = jnp.bfloat16, jnp.float32
    return pl.pallas_call(
        _kernel,
        out_shape=jax.ShapeDtypeStruct((ROWS, COLS), bf16),
        in_specs=[hbm, hbm, hbm, vmem, smem, vmem, hbm, vmem],
        out_specs=vmem,
        scratch_shapes=[
            pltpu.VMEM((NZ, CHUNK, 2 * HSIZE), bf16),
            pltpu.VMEM((NZ, CHUNK, HSIZE), bf16),
            pltpu.VMEM((HSIZE, NZ * CHUNK), bf16),
            pltpu.VMEM((NG, ROWS, HSIZE), bf16),
            pltpu.VMEM((8, ROWS), f32),
            pltpu.VMEM((NG, 8, ROWS), f32),
            pltpu.VMEM((2 * HSIZE, NG * ROWS), bf16),
            pltpu.VMEM((8, STREAM * ROWS), f32),
            pltpu.VMEM((8, STREAM * ROWS), f32),
            pltpu.VMEM((HSIZE, STREAM * ROWS), f32),
            pltpu.VMEM((NY, HSIZE, 2 * ROWS), bf16),
            pltpu.VMEM((FEATS, 2 * ROWS), bf16),
            pltpu.VMEM((NZ, TOKF, FEATS), bf16),
            pltpu.VMEM((TOKF, COLS), bf16),
            pltpu.VMEM((ROWS, OWN), bf16),
            pltpu.VMEM((ROWS, OWN), bf16),
            pltpu.VMEM((2, ROWS, 256), bf16),
            dma((5,)),
            dma((7,)), dma((7,)), dma((7,)), dma((7,)),
            dma((7,)), dma((7,)), dma((7,)), dma((7,)),
            dma((2, 5, 2)), dma((2, 5, 2)),
            dma, dma((4,)),
            dma((2, 5, 2)), dma((2, 5, 2)),
            dma((2, 2)), dma((2,)), dma,
            dma((4,)), dma((4,)),
            dma((4, 2)), dma((4, 2)),
            dma((4, 2)), dma((4, 2)),
            dma((4, 2, 2)), dma((4, 2, 2)),
            dma, dma,
            dma((2,)), dma((2,)),
        ],
        compiler_params=pltpu.CompilerParams(
            collective_id=0, has_side_effects=True, vmem_limit_bytes=58 * 2**20
        ),
    )(queries, keys, values, frame_mask, frame_slot, out_weight, residual, gate.reshape(1, COLS))


def solution(mesh):
    fine = Mesh(mesh.devices.reshape(2, NY, NZ, 2, 2), AXES)
    wide, head = ("xl", "y", "z"), ("xh", "core")
    return jax.shard_map(
        _on_device,
        mesh=fine,
        in_specs=(
            P(wide, head),
            P(wide, head),
            P(wide, head),
            P(wide, None),
            P(),
            P(head, wide),
            P(wide, head),
            P(head),
        ),
        out_specs=P(wide, head),
        check_vma=False,
    )
```

time: 1100 us -> 104 us (0.09)
  waiting for transfers between devices: 894 us -> 0 us
  matrix products: 113 us -> 0 us
  Pallas kernels: 0 us -> 98.8 us
  other arithmetic: 39.4 us -> 0 us
  local copies, waits for them, and re-layouts: 31.3 us -> 4.64 us
  between operations: 13.2 us -> 0.01 us
    all_gather x3 -> x0, waiting for transfers between devices: 723 us -> none  [the longest x1 311 us: on_device(): lax.all_gather(values, 'wide', axis=0, tiled=True)]
    psum x1 -> x0, waiting for transfers between devices: 168 us -> none  [on_device(): summed = lax.psum(partial_terms, 'head')]
    dot_general x25 -> x0, matrix products: 113 us -> none  [the longest x8 49.7 us: attend_block(): jnp.einsum('rht,thd->rhd', weights.astype(jnp.bfloat16), value_block, pre...]
    pallas_call x0 -> x1, Pallas kernels: none -> 98.8 us  [_on_device(): pl.pallas_call(_kernel, out_shape=jax.ShapeDtypeStruct((ROWS, COLS), bf16...]
    reduce_sum x17 -> x0, other arithmetic: 34.4 us -> none  [the longest x8 32.7 us: attend_block(): run_total = run_total * factor + jnp.sum(weights, axis=2)]
    dynamic_slice x32 -> x0, local copies, waits for them, and re-layouts: 26.9 us -> none  [the longest x16 18.1 us: inner(): value_rows = lax.dynamic_slice_in_dim(all_values, offset, block_size, 0)]
  transfers between devices with their start and end apart: 4 -> 0, of which waited for: 4 -> 0; matrix products, arithmetic and copies ran while one was open for 16% -> 0% of each run, Pallas kernels for 0% -> 0%
where the time goes in v2:
time: 104 us; the launch traced here: 103 us
  Pallas kernels  98.8 us (95%)
  local copies, waits for them, and re-layouts  4.64 us (4%)
    pallas_call x1, Pallas kernels, _on_device(): pl.pallas_call(_kernel, out_shape=jax.ShapeDtypeStruct((ROWS, COLS), bf16...  98.8 us
    unnamed x5, local copies, waits for them, and re-layouts  4.64 us

profile of v2, /device:TPU:1, one launch (start us, length us, event | category | flops | bytes accessed | tf_op | source)
XLA Modules:
  0.0 103.5 jit_solution(17354902032890939124)
XLA Ops:
  0.0 0.0 copy-start
  0.0 1.7 %copy.9.mask_ref = s32[384,64]{1,0:T(8,128)} copy(s32[384,64]{0,1:T(8,128)} %param.11) | data formatting | bytes 196608 | tf_op args[3]
  1.7 0.0 copy-done
  1.7 0.8 copy.10.w_ref
  2.6 98.8 %shard_map.82 = bf16[384,1024]{1,0:T(8,128)(2,1)} custom-call(bf16[384,1024]{1,0:T(8,128)(2,1)} %q_ref.1, bf16[64,1024]{1,0:T(8,128)(2,1)} %k_ref.1, bf16[64,1024]{1,0:T(8,128)(2,1)} %v_ref.1, s32[384,64]{1,0:T(8,128)} %copy.9.mask_ref, s32[64]{0:T(128)} %slot_ref.1, bf16[1024,64]{1,0:T(8,128)(2,1)} %copy.10.w_ref, bf16[384,1024]{1,0:T(8,128)(2,1)} %res_ref.1, ...), custom_call_target="tpu_custom_call" | custom-call | tf_op jit(solution)/shard_map/pallas_call | solution.py:500
  101.4 2.1 %copy.12 = bf16[384,1024]{1,0:T(8,128)(2,1)} copy(bf16[384,1024]{1,0:T(8,128)(2,1)} %shard_map.82) | data formatting | bytes 1572864
Async XLA Ops:
  0.0 1.7 %copy-start = (bf16[1024,64]{0,1:T(8,128)(2,1)S(1)}, bf16[1024,64]{0,1:T(8,128)(2,1)}, u32[]{:S(2)}) copy-start(bf16[1024,64]{0,1:T(8,128)(2,1)} %param.13) | copy-start | bytes 393220

commit v3 on v2

--- a/solution.py
+++ b/solution.py
@@ -30,9 +30,9 @@
 
 def _kernel(
     q_ref, k_ref, v_ref, mask_ref, slot_ref, w_ref, res_ref, gate_ref, out_ref,
-    k2, vbuf, vt, qbuf, bnd, bbuf, qt, m_sc, l_sc, acc, satt, att, wt, wown, res, res2, upd,
+    k2, vbuf, vt, qbuf, bnd, bbuf, qt, m_sc, l_sc, acc, satt, att, wt, res, res2, upd, psum,
     loc, ka_s, ka_r, va_s, va_r, q_s, q_r, b_s, b_r, kv_s, kv_r,
-    wx_s, wx_r, wr_s, wr_r, wy_s, wy_r, rl_s,
+    wx_s, wx_r, wr_s, wr_r, wn_s, wn_r, wy_s, wy_r, rl_s,
     t1_s, t1_r, t2_s, t2_r, t3_s, t3_r, sb_s, sb_r, rs_s, rs_r, up_s, up_r,
 ):
     xl, y, z = lax.axis_index("xl"), lax.axis_index("y"), lax.axis_index("z")
@@ -75,10 +75,8 @@
     def own_copy(src, dst, i):
         return pltpu.make_async_copy(src, dst, loc.at[i])
 
-    wown[...] = w_ref[...].T
-    ones = jnp.ones((8, mask_ref.shape[1]), jnp.bfloat16)
-    bnd[...] = lax.dot_general(
-        ones, mask_ref[...].astype(jnp.bfloat16), (((1,), (1,)), ((), ())), preferred_element_type=jnp.float32
+    bnd[...] = jnp.broadcast_to(
+        jnp.sum(mask_ref[...], axis=0, keepdims=True).astype(jnp.float32), (8, ROWS)
     )
     bbuf[PLACE[(0, 0)]] = bnd[...]
     pl.semaphore_wait(bar, len(peers))
@@ -86,8 +84,8 @@
     def feat_cols(h):
         return pl.ds(pl.multiple_of(h * COLS, COLS), COLS)
 
-    wx_copy = remote(wown, wt.at[z, :, feat_cols(head)], wx_s, wx_r.at[head], (ylo, y, z, xl, y // 2))
-    wx_own = pltpu.make_async_copy(wown, wt.at[z, :, feat_cols(head)], wx_r.at[head])
+    wx_copy = remote(w_ref, wt.at[z, :, feat_cols(head)], wx_s, wx_r.at[head], (ylo, y, z, xl, y // 2))
+    wx_own = pltpu.make_async_copy(w_ref, wt.at[z, :, feat_cols(head)], wx_r.at[head])
     wx_is_self = jnp.logical_and(home, xl == xh)
 
     def tok_rows(i):
@@ -187,12 +185,14 @@
             for d in ring_dirs(1, which):
                 self.send(d, 1, which).start()
 
-        def step(self, r, pieces=(0, 1)):
+        def step(self, r, pieces=(0, 1), also=None):
             for which in pieces:
                 for d in ring_dirs(r, which):
                     self.copy(d, r, which, r).wait_recv()
                     if r < 4 and d in ring_dirs(r + 1, which):
                         self.send(d, r + 1, which).start()
+                    if also is not None:
+                        also(d, which)
 
         def end(self):
             for r in range(1, 5):
@@ -204,7 +204,24 @@
         return slice(32 * which, 32 * which + 32)
 
     kv_ring = Ring(lambda slot, w: vbuf.at[slot] if w else k2.at[slot, :, 0:HSIZE], kv_s, kv_r)
-    w_ring = Ring(lambda slot, w: wt.at[slot, half(w)], wr_s, wr_r)
+    def w_rows(parity, which):
+        return pl.ds(pl.multiple_of(32 * parity + 16 * which, 16), 16)
+
+    w_ring = Ring(lambda slot, w: wt.at[slot, w_rows(ylo, w)], wr_s, wr_r)
+
+    def wn_copy(d, r, which, parity):
+        ref = wt.at[lax.rem(z - d * r + 2 * NZ, NZ), w_rows(parity, which)]
+        i = 0 if d == 1 else 1
+        return remote(ref, ref, wn_s.at[i, r, which], wn_r.at[i, r, which], dev(dy=d * (1 - 2 * ylo)))
+
+    def w_step(r, pieces=(0, 1)):
+        w_ring.step(r, pieces, lambda d, which: wn_copy(d, r, which, ylo).start())
+
+    def w_each(act):
+        for r in range(1, 5):
+            for which in range(2):
+                for d in ring_dirs(r, which):
+                    act(d, r, which)
 
     def wy_copy(which, d, s):
         ref = wt.at[z, half(which)]
@@ -262,12 +279,16 @@
             jnp.bfloat16
         )
 
-    for i, (dy, o) in enumerate(PLANE):
-        q_copy(i, dy, o).wait_recv()
-        b_copy(i, dy, o).wait_recv()
-        queries_in(PLACE[(-dy % NY, o)])
-    q_own.wait()
-    queries_in(PLACE[(0, 0)])
+    def queries(first, last):
+        for i, (dy, o) in enumerate(PLANE):
+            p = PLACE[(-dy % NY, o)]
+            if first <= p < last:
+                q_copy(i, dy, o).wait_recv()
+                b_copy(i, dy, o).wait_recv()
+                queries_in(p)
+        if first <= PLACE[(0, 0)] < last:
+            q_own.wait()
+            queries_in(PLACE[(0, 0)])
 
     def vt_cols(slot):
         return pl.ds(pl.multiple_of(slot * CHUNK, CHUNK), CHUNK)
@@ -360,6 +381,7 @@
         satt[dy, :, cols] = (mixed / (total + empty)).astype(jnp.bfloat16)
 
     def attend_block(p):
+        queries(p, p + 1)
         s = jnp.dot(
             k2[...].reshape(NZ * CHUNK, 2 * HSIZE),
             qt[:, p * ROWS : (p + 1) * ROWS],
@@ -371,14 +393,15 @@
         mixed = jnp.dot(vt[...], w.astype(jnp.bfloat16), preferred_element_type=jnp.float32)
         normed(p, mixed, total)
 
+    kv_ring.step(2)
+    relayed()
+    queries(0, STREAM)
     attend(0)
-    kv_ring.step(2)
+    kv_ring.step(3)
+    w_ring.begin(0)
+    w_ring.begin(1)
     attend(1)
     attend(2)
-    relayed()
-    kv_ring.step(3)
-    for which in range(2):
-        w_ring.begin(which)
     attend(3)
     attend(4)
     kv_ring.step(4)
@@ -390,31 +413,50 @@
         normed(p, acc[:, cols], l_sc[0:1, cols])
         if p % 2:
             give(ORDER[p // 2])
-    w_ring.step(1, (0,))
     attend_block(4)
+    w_step(1)
+    pass_on(ORDER[1])
     pass_on(ORDER[0])
-    w_ring.step(1, (1,))
     attend_block(5)
     give(ORDER[2])
-    pass_on(ORDER[1])
     take(ORDER[0])
-    w_ring.step(2, (0,))
     attend_block(6)
+    w_step(2)
     pass_on(ORDER[2])
     take(ORDER[1])
-    w_ring.step(2, (1,))
     attend_block(7)
     give(ORDER[3])
     take_far(ORDER[0])
-    w_ring.step(3, (0,))
+    w_step(3)
     take(ORDER[2])
     pass_on(ORDER[3])
     take_far(ORDER[1])
-    w_ring.step(3, (1,))
+    w_step(4)
+    take_far(ORDER[2])
     take(ORDER[3])
-    take_far(ORDER[2])
     take_far(ORDER[3])
-    w_ring.step(4)
+    w_each(lambda d, r, which: wn_copy(d, r, which, 1 - ylo).wait_recv())
+
+    def side_rows(side):
+        return pl.ds(pl.multiple_of(side * ROWS, ROWS), ROWS)
+
+    def project(i, side, c):
+        total = None
+        for h in (c, 2 + c):
+            w = wt[4 * i : 4 * i + 4, :, feat_cols(h)].reshape(256, COLS)
+            part = jnp.dot(w, att[feat_cols(h), side_rows(side)], preferred_element_type=jnp.float32)
+            total = part if total is None else total + part
+        return total
+
+    def finish(i, side, before):
+        summed = psum[2 * i + (0 if before is res2 else 1)] + project(i, side, 1 - core)
+        scale = jnp.tanh(gate_ref[:, pl.ds(pl.multiple_of(xl * OWN + i * 256, 256), 256)])
+        old = before[:, 256 * i : 256 * i + 256].astype(jnp.float32)
+        return (old + scale * summed.T).astype(jnp.bfloat16)
+
+    for i in range(2):
+        psum[2 * i] = project(i, 1 - xl, core)
+        psum[2 * i + 1] = project(i, xl, core)
     for dy in ORDER:
         for o in range(2):
             for h in range(2):
@@ -422,13 +464,6 @@
     res_in.wait()
     res_out.wait_recv()
 
-    def project(i, side, before, put):
-        w = wt[4 * i : 4 * i + 4].reshape(256, FEATS)
-        rows = pl.ds(pl.multiple_of(side * ROWS, ROWS), ROWS)
-        summed = jnp.dot(w, att[:, rows], preferred_element_type=jnp.float32)
-        scale = jnp.tanh(gate_ref[:, pl.ds(pl.multiple_of(xl * OWN + i * 256, 256), 256)])
-        put((before.astype(jnp.float32) + scale * summed.T).astype(jnp.bfloat16))
-
     def up_copy(i):
         cols = pl.ds(pl.multiple_of(xl * OWN + i * 256, 256), 256)
         return remote(upd.at[i], out_ref.at[:, cols], up_s.at[i], up_r.at[i], partner)
@@ -438,18 +473,10 @@
         return remote(upd.at[i], out_ref.at[:, cols], up_s.at[i], up_r.at[i], partner)
 
     for i in range(2):
-
-        def put_far(x):
-            upd[i] = x
-
-        project(i, 1 - xl, res2[:, 256 * i : 256 * i + 256], put_far)
+        upd[i] = finish(i, 1 - xl, res2)
         up_copy(i).start()
     for i in range(2):
-
-        def put_own(x):
-            out_ref[:, pl.ds(pl.multiple_of(xl * OWN + i * 256, 256), 256)] = x
-
-        project(i, xl, res[:, 256 * i : 256 * i + 256], put_own)
+        out_ref[:, pl.ds(pl.multiple_of(xl * OWN + i * 256, 256), 256)] = finish(i, xl, res)
     for i in range(2):
         up_got(i).wait_recv()
 
@@ -466,6 +493,7 @@
     kv_ring.end()
 
     w_ring.end()
+    w_each(lambda d, r, which: wn_copy(d, r, which, ylo).wait_send())
 
     @pl.when(home)
     def _():
@@ -516,15 +544,16 @@
             pltpu.VMEM((NY, HSIZE, 2 * ROWS), bf16),
             pltpu.VMEM((FEATS, 2 * ROWS), bf16),
             pltpu.VMEM((NZ, TOKF, FEATS), bf16),
-            pltpu.VMEM((TOKF, COLS), bf16),
             pltpu.VMEM((ROWS, OWN), bf16),
             pltpu.VMEM((ROWS, OWN), bf16),
             pltpu.VMEM((2, ROWS, 256), bf16),
+            pltpu.VMEM((4, 256, ROWS), f32),
             dma((5,)),
             dma((7,)), dma((7,)), dma((7,)), dma((7,)),
             dma((7,)), dma((7,)), dma((7,)), dma((7,)),
             dma((2, 5, 2)), dma((2, 5, 2)),
             dma, dma((4,)),
+            dma((2, 5, 2)), dma((2, 5, 2)),
             dma((2, 5, 2)), dma((2, 5, 2)),
             dma((2, 2)), dma((2,)), dma,
             dma((4,)), dma((4,)),
@@ -537,7 +566,7 @@
         compiler_params=pltpu.CompilerParams(
             collective_id=0, has_side_effects=True, vmem_limit_bytes=58 * 2**20
         ),
-    )(queries, keys, values, frame_mask, frame_slot, out_weight, residual, gate.reshape(1, COLS))
+    )(queries, keys, values, frame_mask.T, frame_slot, out_weight.T, residual, gate.reshape(1, COLS))
 
 
 def solution(mesh):

time: 104 us -> 99 us (0.952)
  Pallas kernels: 98.8 us -> 95.9 us
  local copies, waits for them, and re-layouts: 4.64 us -> 2.06 us
    pallas_call x1, Pallas kernels: 98.8 us -> 95.9 us  [_on_device(): pl.pallas_call(_kernel, out_shape=jax.ShapeDtypeStruct((ROWS, COLS), bf16...]
    unnamed x5 -> x1, local copies, waits for them, and re-layouts: 4.64 us -> 2.06 us
where the time goes in v3:
time: 99 us; the launch traced here: 98 us
  Pallas kernels  95.9 us (97%)
  local copies, waits for them, and re-layouts  2.06 us (2%)
    pallas_call x1, Pallas kernels, _on_device(): pl.pallas_call(_kernel, out_shape=jax.ShapeDtypeStruct((ROWS, COLS), bf16...  95.9 us
    unnamed x1, local copies, waits for them, and re-layouts  2.06 us

profile of v3, /device:TPU:1, one launch (start us, length us, event | category | flops | bytes accessed | tf_op | source)
XLA Modules:
  0.0 98.0 jit_solution(13821876780624541723)
XLA Ops:
  0.0 95.9 %shard_map.82 = bf16[384,1024]{1,0:T(8,128)(2,1)} custom-call(bf16[384,1024]{1,0:T(8,128)(2,1)} %q_ref.1, bf16[64,1024]{1,0:T(8,128)(2,1)} %k_ref.1, bf16[64,1024]{1,0:T(8,128)(2,1)} %v_ref.1, s32[64,384]{1,0:T(8,128)} %bitcast.4, s32[64]{0:T(128)} %slot_ref.1, bf16[64,1024]{1,0:T(8,128)(2,1)} %bitcast.3, bf16[384,1024]{1,0:T(8,128)(2,1)} %res_ref.1, ...), custom_call_target="tpu_custom_call" | custom-call | tf_op jit(solution)/shard_map/pallas_call | solution.py:528
  95.9 2.1 %copy.10 = bf16[384,1024]{1,0:T(8,128)(2,1)} copy(bf16[384,1024]{1,0:T(8,128)(2,1)} %shard_map.82) | data formatting | bytes 1572864

commit v4 on v3

--- a/solution.py
+++ b/solution.py
@@ -147,7 +147,6 @@
         b_copy(i, dy, o).start()
     q_own.start()
     res_in.start()
-    res_out.start()
 
     lane = lax.broadcasted_iota(jnp.int32, (TOKF, HSIZE), 1)
 
@@ -396,17 +395,16 @@
     kv_ring.step(2)
     relayed()
     queries(0, STREAM)
+    res_out.start()
     attend(0)
+    attend(1)
+    attend(2)
     kv_ring.step(3)
     w_ring.begin(0)
     w_ring.begin(1)
-    attend(1)
-    attend(2)
-    attend(3)
-    attend(4)
+    for n in range(3, 7):
+        attend(n)
     kv_ring.step(4)
-    attend(5)
-    attend(6)
     attend(7)
     for p in range(STREAM):
         cols = slice(p * ROWS, (p + 1) * ROWS)
@@ -423,9 +421,9 @@
     attend_block(6)
     w_step(2)
     pass_on(ORDER[2])
-    take(ORDER[1])
     attend_block(7)
     give(ORDER[3])
+    take(ORDER[1])
     take_far(ORDER[0])
     w_step(3)
     take(ORDER[2])

time: 99 us -> 98.5 us (level)
  no operation moved by 1% of the time
where the time goes in v4:
time: 98.5 us; the launch traced here: 98.4 us
  Pallas kernels  96.3 us (98%)
  local copies, waits for them, and re-layouts  2.06 us (2%)
    pallas_call x1, Pallas kernels, _on_device(): pl.pallas_call(_kernel, out_shape=jax.ShapeDtypeStruct((ROWS, COLS), bf16...  96.3 us
    unnamed x1, local copies, waits for them, and re-layouts  2.06 us

profile of v4, /device:TPU:1, one launch (start us, length us, event | category | flops | bytes accessed | tf_op | source)
XLA Modules:
  0.0 98.4 jit_solution(17368652035280017530)
XLA Ops:
  0.0 96.3 %shard_map.82 = bf16[384,1024]{1,0:T(8,128)(2,1)} custom-call(bf16[384,1024]{1,0:T(8,128)(2,1)} %q_ref.1, bf16[64,1024]{1,0:T(8,128)(2,1)} %k_ref.1, bf16[64,1024]{1,0:T(8,128)(2,1)} %v_ref.1, s32[64,384]{1,0:T(8,128)} %bitcast.4, s32[64]{0:T(128)} %slot_ref.1, bf16[64,1024]{1,0:T(8,128)(2,1)} %bitcast.3, bf16[384,1024]{1,0:T(8,128)(2,1)} %res_ref.1, ...), custom_call_target="tpu_custom_call" | custom-call | tf_op jit(solution)/shard_map/pallas_call | solution.py:526
  96.3 2.1 %copy.10 = bf16[384,1024]{1,0:T(8,128)(2,1)} copy(bf16[384,1024]{1,0:T(8,128)(2,1)} %shard_map.82) | data formatting | bytes 1572864
